TPU v7x, 256 devices: a whole 4x4x8 slice. The times are simulated.
256 devices in a mesh: section: 8 (over z), sp: 8 (over y, x_hi), prompt: 4 (over x_lo, core).
Axes of the slice: x: 4 (x_hi: 2, x_lo: 2; x = x_hi * 2 + x_lo), y: 4, z: 8, core: 2. Of those that a mesh axis runs over, the one named last changes fastest.
Arguments:
- latents: bfloat16 [32, 64, 3072], P('prompt', 'sp'), parts along dimension 0, may hold values from -6 to 6
- offsets: int32 [32], P('prompt'), parts along dimension 0, may hold values from 0 to 448, as said below
- norm_gain: float32 [8, 3072], P('section'), may hold values from 0.5 to 2
- w_qkv: bfloat16 [8, 3072, 3, 2048], P('section', None, None, 'sp'), may hold values from -0.109375 to 0.109375
- qk_gain: float32 [8, 2, 128], P('section'), may hold values from 0.5 to 2
- w_out: bfloat16 [8, 2048, 3072], P('section', 'sp'), may hold values from -0.125 to 0.125
- kv_cache: bfloat16 [8, 2, 2048, 2048], P('section', None, 'prompt', 'sp'), parts along dimension 2, may hold values from -24 to 24
Outputs:
- section_out: bfloat16 [8, 32, 64, 3072], P('section', 'prompt', 'sp'), parts along dimension 1
- kv_out: bfloat16 [8, 2, 2048, 2048], P('section', None, 'prompt', 'sp'), parts along dimension 2
There are 4 independent parts, one for each index of `prompt`. A program takes and returns all parts, laid end to end along the dimension named above; an argument that names none is the same for every part. Nothing has to cross between parts.
Inputs may be any that keep to these rules, and one draw needn't show every extreme that they name: `offsets`: each multiple of 64 below 512 appears once.
All inputs are finite; a program needn't handle non-finite values.
Results may differ from a plain program's by a relative error of at most 0.04.
Values may be sent and summed in bfloat16 or wider, within the bound.
No kernel may reach another device: no remote copies, remote signals or barrier semaphores. Data moves between devices by JAX's collectives and lax.ppermute only.
A program may use at most 64 MiB of HBM per device.

v0:
```python
import math

import jax
import jax.numpy as jnp
from jax import lax
from jax.sharding import PartitionSpec as P

EPS = 1e-06


def shifted(value, axis, steps):
    count = lax.axis_size(axis)
    first, last = (max(0, -steps), min(count, count - steps))
    return lax.ppermute(value, axis, [(source, source + steps) for source in range(first, last)])


def rms_scale(values):
    return values * lax.rsqrt(jnp.mean(values * values, axis=-1, keepdims=True) + EPS)


def on_device(latents, offsets, norm_gain, w_qkv, qk_gain, w_out, kv_cache):
    group_count = lax.axis_size("sp")
    section_count = lax.axis_size("section")
    section_no = lax.axis_index("section")
    patch_count = offsets.shape[0]
    shard_rows = latents.shape[1]
    patch_rows = shard_rows * group_count
    model_width = latents.shape[2]
    local_width = w_out.shape[1]
    head_dim = qk_gain.shape[2]
    local_heads = local_width // head_dim
    seq_len = kv_cache.shape[2]
    gain_row = norm_gain[0]
    w_project = w_qkv[0].reshape(model_width, 3 * local_width)
    w_output = w_out[0]

    def attend(projected, kv_state, offset, active):
        projected = projected.reshape(patch_rows, 3, local_heads, head_dim)
        queries = (rms_scale(projected[:, 0]) * qk_gain[0, 0]).astype(jnp.bfloat16)
        keys_new = (rms_scale(projected[:, 1]) * qk_gain[0, 1]).astype(jnp.bfloat16)
        values_new = projected[:, 2].astype(jnp.bfloat16)
        fresh_kv = jnp.stack([keys_new, values_new]).reshape(2, patch_rows, local_width)
        corner = (jnp.int32(0), offset, jnp.int32(0))
        previous = lax.dynamic_slice(kv_state, corner, (2, patch_rows, local_width))
        kv_state = lax.dynamic_update_slice(kv_state, jnp.where(active, fresh_kv, previous), corner)
        key_rows = kv_state[0].reshape(seq_len, local_heads, head_dim)
        value_rows = kv_state[1].reshape(seq_len, local_heads, head_dim)
        scores = jnp.einsum(
            "phd,shd->hps", queries, key_rows, preferred_element_type=jnp.float32
        ) / math.sqrt(head_dim)
        weights = jax.nn.softmax(scores, axis=-1).astype(jnp.bfloat16)
        mixture = jnp.einsum(
            "hps,shd->phd", weights, value_rows, preferred_element_type=jnp.float32
        )
        return (mixture.astype(jnp.bfloat16).reshape(patch_rows, local_width), kv_state)

    def tick(tick_no, carry):
        inflow, kv_state, produced = carry
        slot_no = tick_no - section_no
        active = (slot_no >= 0) & (slot_no < patch_count)
        slot_no = jnp.clip(slot_no, 0, patch_count - 1)
        offset = offsets[slot_no]
        patch_index = offset // patch_rows
        source = lax.dynamic_index_in_dim(latents, patch_index, 0, keepdims=False)
        current = jnp.where(section_no == 0, source, inflow)
        normed = (rms_scale(current.astype(jnp.float32)) * gain_row).astype(jnp.bfloat16)
        projected = jnp.dot(
            lax.all_gather(normed, "sp", axis=0, tiled=True),
            w_project,
            preferred_element_type=jnp.float32,
        )
        mixture, kv_state = attend(projected, kv_state, offset, active)
        attended = lax.psum_scatter(
            jnp.dot(mixture, w_output, preferred_element_type=jnp.float32).astype(jnp.bfloat16),
            "sp",
            scatter_dimension=0,
            tiled=True,
        ).astype(jnp.float32)
        result = (current.astype(jnp.float32) + attended).astype(jnp.bfloat16)
        stored = lax.dynamic_index_in_dim(produced, patch_index, 0, keepdims=False)
        produced = lax.dynamic_update_index_in_dim(
            produced, jnp.where(active, result, stored), patch_index, 0
        )
        inflow = shifted(result, "section", 1)
        return (inflow, kv_state, produced)

    start_flow = jnp.zeros((shard_rows, model_width), jnp.bfloat16)
    produced = jnp.zeros_like(latents)
    carry = (start_flow, kv_cache[0], produced)
    carry = lax.fori_loop(0, patch_count + section_count - 1, tick, carry)
    return (carry[2][None], carry[1][None])


def solution(mesh):
    in_specs = (
        P("prompt", "sp", None),
        P("prompt"),
        P("section", None),
        P("section", None, None, "sp"),
        P("section", None, None),
        P("section", "sp", None),
        P("section", None, "prompt", "sp"),
    )
    out_specs = (P("section", "prompt", "sp", None), P("section", None, "prompt", "sp"))
    return jax.shard_map(
        on_device, mesh=mesh, in_specs=in_specs, out_specs=out_specs, check_vma=False
    )
```

profile of v0, /device:TPU:96, one launch (start us, length us, event | category | flops | bytes accessed | tf_op | source)
XLA Modules:
  0.0 1987.1 jit_solution(13221809061456741121)
XLA Ops:
  21.0 1958.6 %while.19 = (s32[]{:T(128)}, bf16[8,3072]{1,0:T(8,128)(2,1)S(1)}, bf16[2,512,256]{1,2,0:T(8,128)(2,1)S(1)}, bf16[8,8,3072]{2,1,0:T(8,128)(2,1)S(1)}, pred[]{:T(5...) while((s32[]{:T(128)}, bf16[8,3072]{1,0:T(8,128)(2,1)S(1)}, ...), condition=%wide.region_7.8_spmd, body=%wide.region_0.7_spmd.sunk | while | flops 437462432 | bytes 13688498 | solution.py:90
  25.3 35.5 %all_gather.11 = bf16[64,3072]{1,0:T(8,128)(2,1)S(1)} all-gather(bf16[8,3072]{1,0:T(8,128)(2,1)S(1)} %fusion.52), channel_id=1, replica_groups=mesh['section'=8,'sp'=8,'prompt'=4] {'sp'}, dimensions={0}, use_global_device_ids=true | all-gather | bytes 442368 | tf_op jit(solution)/shard_map/while/body/eval_jaxpr/all_gather | solution.py:68
  69.0 77.1 %reduce-scatter.2.cloned.1.call-done = bf16[8,3072]{1,0:T(8,128)(2,1)} async-done(((bf16[64,3072]{1,0:T(8,128)(2,1)}), bf16[8,3072]{1,0:T(8,128)(2,1)}) %reduce-scatter.2.cloned.1.call-update) | async-done | bytes 49168 | tf_op jit(solution)/shard_map/while/body/eval_jaxpr/reduce_scatter | solution.py:73
  201.2 75.6 %reduce-scatter.2.cloned.1.call-done = bf16[8,3072]{1,0:T(8,128)(2,1)} async-done(((bf16[64,3072]{1,0:T(8,128)(2,1)}), bf16[8,3072]{1,0:T(8,128)(2,1)}) %reduce-scatter.2.cloned.1.call-update) | async-done | bytes 49168 | tf_op jit(solution)/shard_map/while/body/eval_jaxpr/reduce_scatter | solution.py:73
  288.2 35.4 %all_gather.11 = bf16[64,3072]{1,0:T(8,128)(2,1)S(1)} all-gather(bf16[8,3072]{1,0:T(8,128)(2,1)S(1)} %fusion.52), channel_id=1, replica_groups=mesh['section'=8,'sp'=8,'prompt'=4] {'sp'}, dimensions={0}, use_global_device_ids=true | all-gather | bytes 442368 | tf_op jit(solution)/shard_map/while/body/eval_jaxpr/all_gather | solution.py:68
  331.8 75.5 %reduce-scatter.2.cloned.1.call-done = bf16[8,3072]{1,0:T(8,128)(2,1)} async-done(((bf16[64,3072]{1,0:T(8,128)(2,1)}), bf16[8,3072]{1,0:T(8,128)(2,1)}) %reduce-scatter.2.cloned.1.call-update) | async-done | bytes 49168 | tf_op jit(solution)/shard_map/while/body/eval_jaxpr/reduce_scatter | solution.py:73
  462.3 75.6 %reduce-scatter.2.cloned.1.call-done = bf16[8,3072]{1,0:T(8,128)(2,1)} async-done(((bf16[64,3072]{1,0:T(8,128)(2,1)}), bf16[8,3072]{1,0:T(8,128)(2,1)}) %reduce-scatter.2.cloned.1.call-update) | async-done | bytes 49168 | tf_op jit(solution)/shard_map/while/body/eval_jaxpr/reduce_scatter | solution.py:73
  549.3 35.4 %all_gather.11 = bf16[64,3072]{1,0:T(8,128)(2,1)S(1)} all-gather(bf16[8,3072]{1,0:T(8,128)(2,1)S(1)} %fusion.52), channel_id=1, replica_groups=mesh['section'=8,'sp'=8,'prompt'=4] {'sp'}, dimensions={0}, use_global_device_ids=true | all-gather | bytes 442368 | tf_op jit(solution)/shard_map/while/body/eval_jaxpr/all_gather | solution.py:68
  592.9 75.3 %reduce-scatter.2.cloned.1.call-done = bf16[8,3072]{1,0:T(8,128)(2,1)} async-done(((bf16[64,3072]{1,0:T(8,128)(2,1)}), bf16[8,3072]{1,0:T(8,128)(2,1)}) %reduce-scatter.2.cloned.1.call-update) | async-done | bytes 49168 | tf_op jit(solution)/shard_map/while/body/eval_jaxpr/reduce_scatter | solution.py:73
  679.8 35.4 %all_gather.11 = bf16[64,3072]{1,0:T(8,128)(2,1)S(1)} all-gather(bf16[8,3072]{1,0:T(8,128)(2,1)S(1)} %fusion.52), channel_id=1, replica_groups=mesh['section'=8,'sp'=8,'prompt'=4] {'sp'}, dimensions={0}, use_global_device_ids=true | all-gather | bytes 442368 | tf_op jit(solution)/shard_map/while/body/eval_jaxpr/all_gather | solution.py:68
  723.9 74.9 %reduce-scatter.2.cloned.1.call-done = bf16[8,3072]{1,0:T(8,128)(2,1)} async-done(((bf16[64,3072]{1,0:T(8,128)(2,1)}), bf16[8,3072]{1,0:T(8,128)(2,1)}) %reduce-scatter.2.cloned.1.call-update) | async-done | bytes 49168 | tf_op jit(solution)/shard_map/while/body/eval_jaxpr/reduce_scatter | solution.py:73
  854.2 74.8 %reduce-scatter.2.cloned.1.call-done = bf16[8,3072]{1,0:T(8,128)(2,1)} async-done(((bf16[64,3072]{1,0:T(8,128)(2,1)}), bf16[8,3072]{1,0:T(8,128)(2,1)}) %reduce-scatter.2.cloned.1.call-update) | async-done | bytes 49168 | tf_op jit(solution)/shard_map/while/body/eval_jaxpr/reduce_scatter | solution.py:73
  940.5 35.4 %all_gather.11 = bf16[64,3072]{1,0:T(8,128)(2,1)S(1)} all-gather(bf16[8,3072]{1,0:T(8,128)(2,1)S(1)} %fusion.52), channel_id=1, replica_groups=mesh['section'=8,'sp'=8,'prompt'=4] {'sp'}, dimensions={0}, use_global_device_ids=true | all-gather | bytes 442368 | tf_op jit(solution)/shard_map/while/body/eval_jaxpr/all_gather | solution.py:68
  984.1 75.2 %reduce-scatter.2.cloned.1.call-done = bf16[8,3072]{1,0:T(8,128)(2,1)} async-done(((bf16[64,3072]{1,0:T(8,128)(2,1)}), bf16[8,3072]{1,0:T(8,128)(2,1)}) %reduce-scatter.2.cloned.1.call-update) | async-done | bytes 49168 | tf_op jit(solution)/shard_map/while/body/eval_jaxpr/reduce_scatter | solution.py:73
  1114.8 75.0 %reduce-scatter.2.cloned.1.call-done = bf16[8,3072]{1,0:T(8,128)(2,1)} async-done(((bf16[64,3072]{1,0:T(8,128)(2,1)}), bf16[8,3072]{1,0:T(8,128)(2,1)}) %reduce-scatter.2.cloned.1.call-update) | async-done | bytes 49168 | tf_op jit(solution)/shard_map/while/body/eval_jaxpr/reduce_scatter | solution.py:73
  1244.8 75.2 %reduce-scatter.2.cloned.1.call-done = bf16[8,3072]{1,0:T(8,128)(2,1)} async-done(((bf16[64,3072]{1,0:T(8,128)(2,1)}), bf16[8,3072]{1,0:T(8,128)(2,1)}) %reduce-scatter.2.cloned.1.call-update) | async-done | bytes 49168 | tf_op jit(solution)/shard_map/while/body/eval_jaxpr/reduce_scatter | solution.py:73
  1331.5 35.4 %all_gather.11 = bf16[64,3072]{1,0:T(8,128)(2,1)S(1)} all-gather(bf16[8,3072]{1,0:T(8,128)(2,1)S(1)} %fusion.52), channel_id=1, replica_groups=mesh['section'=8,'sp'=8,'prompt'=4] {'sp'}, dimensions={0}, use_global_device_ids=true | all-gather | bytes 442368 | tf_op jit(solution)/shard_map/while/body/eval_jaxpr/all_gather | solution.py:68
  1375.6 74.4 %reduce-scatter.2.cloned.1.call-done = bf16[8,3072]{1,0:T(8,128)(2,1)} async-done(((bf16[64,3072]{1,0:T(8,128)(2,1)}), bf16[8,3072]{1,0:T(8,128)(2,1)}) %reduce-scatter.2.cloned.1.call-update) | async-done | bytes 49168 | tf_op jit(solution)/shard_map/while/body/eval_jaxpr/reduce_scatter | solution.py:73
  1505.6 75.0 %reduce-scatter.2.cloned.1.call-done = bf16[8,3072]{1,0:T(8,128)(2,1)} async-done(((bf16[64,3072]{1,0:T(8,128)(2,1)}), bf16[8,3072]{1,0:T(8,128)(2,1)}) %reduce-scatter.2.cloned.1.call-update) | async-done | bytes 49168 | tf_op jit(solution)/shard_map/while/body/eval_jaxpr/reduce_scatter | solution.py:73
  1592.0 35.4 %all_gather.11 = bf16[64,3072]{1,0:T(8,128)(2,1)S(1)} all-gather(bf16[8,3072]{1,0:T(8,128)(2,1)S(1)} %fusion.52), channel_id=1, replica_groups=mesh['section'=8,'sp'=8,'prompt'=4] {'sp'}, dimensions={0}, use_global_device_ids=true | all-gather | bytes 442368 | tf_op jit(solution)/shard_map/while/body/eval_jaxpr/all_gather | solution.py:68
  1636.2 75.0 %reduce-scatter.2.cloned.1.call-done = bf16[8,3072]{1,0:T(8,128)(2,1)} async-done(((bf16[64,3072]{1,0:T(8,128)(2,1)}), bf16[8,3072]{1,0:T(8,128)(2,1)}) %reduce-scatter.2.cloned.1.call-update) | async-done | bytes 49168 | tf_op jit(solution)/shard_map/while/body/eval_jaxpr/reduce_scatter | solution.py:73
  1722.6 35.4 %all_gather.11 = bf16[64,3072]{1,0:T(8,128)(2,1)S(1)} all-gather(bf16[8,3072]{1,0:T(8,128)(2,1)S(1)} %fusion.52), channel_id=1, replica_groups=mesh['section'=8,'sp'=8,'prompt'=4] {'sp'}, dimensions={0}, use_global_device_ids=true | all-gather | bytes 442368 | tf_op jit(solution)/shard_map/while/body/eval_jaxpr/all_gather | solution.py:68
  1766.8 75.0 %reduce-scatter.2.cloned.1.call-done = bf16[8,3072]{1,0:T(8,128)(2,1)} async-done(((bf16[64,3072]{1,0:T(8,128)(2,1)}), bf16[8,3072]{1,0:T(8,128)(2,1)}) %reduce-scatter.2.cloned.1.call-update) | async-done | bytes 49168 | tf_op jit(solution)/shard_map/while/body/eval_jaxpr/reduce_scatter | solution.py:73
  1897.2 75.1 %reduce-scatter.2.cloned.1.call-done = bf16[8,3072]{1,0:T(8,128)(2,1)} async-done(((bf16[64,3072]{1,0:T(8,128)(2,1)}), bf16[8,3072]{1,0:T(8,128)(2,1)}) %reduce-scatter.2.cloned.1.call-update) | async-done | bytes 49168 | tf_op jit(solution)/shard_map/while/body/eval_jaxpr/reduce_scatter | solution.py:73
  (490 shorter events, 499.8 us)
Async XLA Ops:
  21.0 125.1 %reduce-scatter.2.cloned.1.call-start = ((), (), s32[]{:S(2)}) async-start(), calls=%async_computation.1 | async-start | bytes 442368 | tf_op jit(solution)/shard_map/while/body/eval_jaxpr/reduce_scatter | solution.py:73
  147.0 6.4 collective-permute-start
  153.4 123.3 %reduce-scatter.2.cloned.1.call-start = ((), (), s32[]{:S(2)}) async-start(), calls=%async_computation.1 | async-start | bytes 442368 | tf_op jit(solution)/shard_map/while/body/eval_jaxpr/reduce_scatter | solution.py:73
  277.6 6.4 collective-permute-start
  284.0 123.3 %reduce-scatter.2.cloned.1.call-start = ((), (), s32[]{:S(2)}) async-start(), calls=%async_computation.1 | async-start | bytes 442368 | tf_op jit(solution)/shard_map/while/body/eval_jaxpr/reduce_scatter | solution.py:73
  408.1 6.4 collective-permute-start
  414.5 123.3 %reduce-scatter.2.cloned.1.call-start = ((), (), s32[]{:S(2)}) async-start(), calls=%async_computation.1 | async-start | bytes 442368 | tf_op jit(solution)/shard_map/while/body/eval_jaxpr/reduce_scatter | solution.py:73
  545.1 123.2 %reduce-scatter.2.cloned.1.call-start = ((), (), s32[]{:S(2)}) async-start(), calls=%async_computation.1 | async-start | bytes 442368 | tf_op jit(solution)/shard_map/while/body/eval_jaxpr/reduce_scatter | solution.py:73
  669.1 6.4 collective-permute-start
  675.5 123.3 %reduce-scatter.2.cloned.1.call-start = ((), (), s32[]{:S(2)}) async-start(), calls=%async_computation.1 | async-start | bytes 442368 | tf_op jit(solution)/shard_map/while/body/eval_jaxpr/reduce_scatter | solution.py:73
  799.6 6.4 collective-permute-start
  806.0 123.0 %reduce-scatter.2.cloned.1.call-start = ((), (), s32[]{:S(2)}) async-start(), calls=%async_computation.1 | async-start | bytes 442368 | tf_op jit(solution)/shard_map/while/body/eval_jaxpr/reduce_scatter | solution.py:73
  929.9 6.4 collective-permute-start
  936.3 123.0 %reduce-scatter.2.cloned.1.call-start = ((), (), s32[]{:S(2)}) async-start(), calls=%async_computation.1 | async-start | bytes 442368 | tf_op jit(solution)/shard_map/while/body/eval_jaxpr/reduce_scatter | solution.py:73
  1066.5 123.3 %reduce-scatter.2.cloned.1.call-start = ((), (), s32[]{:S(2)}) async-start(), calls=%async_computation.1 | async-start | bytes 442368 | tf_op jit(solution)/shard_map/while/body/eval_jaxpr/reduce_scatter | solution.py:73
  1197.0 123.0 %reduce-scatter.2.cloned.1.call-start = ((), (), s32[]{:S(2)}) async-start(), calls=%async_computation.1 | async-start | bytes 442368 | tf_op jit(solution)/shard_map/while/body/eval_jaxpr/reduce_scatter | solution.py:73
  1320.8 6.4 collective-permute-start
  1327.3 122.8 %reduce-scatter.2.cloned.1.call-start = ((), (), s32[]{:S(2)}) async-start(), calls=%async_computation.1 | async-start | bytes 442368 | tf_op jit(solution)/shard_map/while/body/eval_jaxpr/reduce_scatter | solution.py:73
  1450.8 6.4 collective-permute-start
  1457.3 123.3 %reduce-scatter.2.cloned.1.call-start = ((), (), s32[]{:S(2)}) async-start(), calls=%async_computation.1 | async-start | bytes 442368 | tf_op jit(solution)/shard_map/while/body/eval_jaxpr/reduce_scatter | solution.py:73
  1581.4 6.4 collective-permute-start
  1587.8 123.3 %reduce-scatter.2.cloned.1.call-start = ((), (), s32[]{:S(2)}) async-start(), calls=%async_computation.1 | async-start | bytes 442368 | tf_op jit(solution)/shard_map/while/body/eval_jaxpr/reduce_scatter | solution.py:73
  1718.4 123.4 %reduce-scatter.2.cloned.1.call-start = ((), (), s32[]{:S(2)}) async-start(), calls=%async_computation.1 | async-start | bytes 442368 | tf_op jit(solution)/shard_map/while/body/eval_jaxpr/reduce_scatter | solution.py:73
  1849.0 123.4 %reduce-scatter.2.cloned.1.call-start = ((), (), s32[]{:S(2)}) async-start(), calls=%async_computation.1 | async-start | bytes 442368 | tf_op jit(solution)/shard_map/while/body/eval_jaxpr/reduce_scatter | solution.py:73
  (12 other events, 74.4 us)
Sparse Core Ops, SparseCore 0:
  69.1 76.9 reduce-scatter.1
  201.3 75.4 reduce-scatter.1
  331.9 75.3 reduce-scatter.1
  462.4 75.4 reduce-scatter.1
  593.0 75.2 reduce-scatter.1
  724.0 74.7 reduce-scatter.1
  854.3 74.6 reduce-scatter.1
  984.2 75.0 reduce-scatter.1
  1114.9 74.8 reduce-scatter.1
  1244.9 75.0 reduce-scatter.1
  1375.7 74.2 reduce-scatter.1
  1505.7 74.8 reduce-scatter.1
  1636.3 74.8 reduce-scatter.1
  1766.9 74.8 reduce-scatter.1
  1897.3 74.9 reduce-scatter.1
where the time goes:
time: 1990 us
  waiting for transfers between devices  1150 us (58%)
  blocking collectives  531 us (27%)
  matrix products  73.1 us (4%)
  starting transfers between devices  70.1 us (4%)
  loops' own time  61.3 us (3%)
  local copies, waits for them, and re-layouts  42.4 us (2%)
  other arithmetic  40.8 us (2%)
    reduce_scatter x15, waiting for transfers between devices, tick(): lax.psum_scatter(jnp.dot(mixture, w_output, preferred_element_type=jnp.fl...  1130 us
    all_gather x15, blocking collectives, tick(): lax.all_gather(normed, 'sp', axis=0, tiled=True)  531 us
    ppermute x15, starting transfers between devices, shifted(): lax.ppermute(value, axis, [(source, source + steps) for source in range(f...  70.1 us
    another operation x1, loops' own time, on_device(): carry = lax.fori_loop(0, patch_count + section_count - 1, tick, carry)  61.3 us
    dot_general x15, matrix products, tick(): jnp.dot(lax.all_gather(normed, 'sp', axis=0, tiled=True), w_project, pref...  48.7 us
  transfers between devices with their start and end apart: 30, of which 30 were waited for; matrix products, arithmetic and copies ran while one was open for 0% of the time, Pallas kernels for 0%

commit v1 on v0

v1 whole, which is shorter than its diff:
```python
import math

import jax
import jax.numpy as jnp
from jax import lax
from jax.experimental import pallas as pl
from jax.experimental.pallas import tpu as pltpu
from jax.sharding import PartitionSpec as P

EPS = 1e-06
CHUNK = 2
OUT_BLOCK = 512
MIB = 1024 * 1024
BF16, F32 = jnp.bfloat16, jnp.float32
VMEM = pl.BlockSpec(memory_space=pltpu.VMEM)
SMEM = pl.BlockSpec(memory_space=pltpu.SMEM)


def onward(value, steps=1):
    count = lax.axis_size("section")
    return lax.ppermute(value, "section", [(i, (i + steps) % count) for i in range(count)])


def spread(value):
    count = lax.axis_size("sp")
    copies = jnp.broadcast_to(value[None], (count,) + value.shape)
    return lax.all_to_all(copies, "sp", 0, 0)


def cost(macs, size):
    return pl.CostEstimate(flops=2 * macs, bytes_accessed=size, transcendentals=0)


def order_kernel(patch_rows, plan, latents, ordered):
    for j in range(latents.shape[0]):
        ordered[j] = latents[plan[j] // patch_rows]


def order_call(patch_rows, plan, latents):
    return pl.pallas_call(
        lambda *refs: order_kernel(patch_rows, *refs),
        out_shape=jax.ShapeDtypeStruct(latents.shape, latents.dtype),
        in_specs=[SMEM, VMEM],
        out_specs=VMEM,
        compiler_params=pltpu.CompilerParams(vmem_limit_bytes=4 * MIB),
    )(plan, latents)


def block_kernel(tick, sections, patch_rows, entry, projects, finishes, *refs):
    refs = list(refs)
    plan, gain, qk_gain, w_project, kv_in, kept_in = refs[:6]
    del refs[:6]
    if projects:
        gathered, x_before, w_before = refs[:3]
        del refs[:3]
    if entry is not None:
        first = refs.pop(0)
    if finishes:
        w_last = refs.pop(0)
    x_out, mixture_out, kv_out, kept_out = refs[:4]
    del refs[:4]
    if finishes:
        terms_out = refs.pop(0)
    normed, x_wide = refs[:2]
    rows, width = x_out.shape
    local_width = kv_out.shape[2]
    head_dim = qk_gain.shape[1]
    chunks = kept_out.shape[0]
    shard_rows = kept_out.shape[2]
    patches = chunks * CHUNK
    section_no, group_no = plan[patches], plan[patches + 1]
    blocks = [slice(i, i + OUT_BLOCK) for i in range(0, width, OUT_BLOCK)]

    kv_out[...] = kv_in[...]
    kept_out[...] = kept_in[...]
    if projects:
        mixed = refs[2]
        for i in range(gathered.shape[0]):
            mixed[:, i * local_width : (i + 1) * local_width] = gathered[i]
        for cols in blocks:
            attended = jnp.dot(mixed[...], w_before[:, cols], preferred_element_type=F32)
            x = x_before[:, cols].astype(F32) + attended
            x_wide[:, cols] = x.astype(BF16).astype(F32)
        block_kept = jnp.where(section_no == 0, sections, section_no)
        slot_kept = tick - block_kept

        @pl.when((slot_kept >= 0) & (slot_kept < chunks))
        def _():
            for i in range(CHUNK):
                at = pl.multiple_of(i * patch_rows + group_no * shard_rows, shard_rows)
                kept_out[slot_kept, i] = x_wide[pl.ds(at, shard_rows), :].astype(BF16)

    def enter():
        for i in range(CHUNK):
            for g in range(first.shape[0]):
                at = i * patch_rows + g * shard_rows
                x_wide[at : at + shard_rows, :] = first[g, entry + i].astype(F32)

    if entry is not None:
        if projects:
            pl.when(section_no == 0)(enter)
        else:
            enter()

    squares = jnp.zeros((rows, 1), F32)
    for cols in blocks:
        x = x_wide[:, cols]
        squares += jnp.sum(x * x, axis=-1, keepdims=True)
        x_out[:, cols] = x.astype(BF16)
    scale = lax.rsqrt(squares / width + EPS)
    for cols in blocks:
        normed[:, cols] = (x_wide[:, cols] * scale * gain[:, cols]).astype(BF16)

    def projected(i):
        return jnp.dot(normed[...], w_project[i], preferred_element_type=F32)

    def head_norm(values, gains):
        parts = []
        for h in range(local_width // head_dim):
            part = values[:, h * head_dim : (h + 1) * head_dim]
            part = part * lax.rsqrt(jnp.mean(part * part, axis=-1, keepdims=True) + EPS)
            parts.append((part * gains).astype(BF16))
        return parts

    queries = head_norm(projected(0), qk_gain[0:1, :])
    keys_new = jnp.concatenate(head_norm(projected(1), qk_gain[1:2, :]), axis=1)
    values_new = projected(2).astype(BF16)
    slot = tick - section_no
    active = (slot >= 0) & (slot < chunks)
    turn = jnp.clip(slot, 0, chunks - 1) * CHUNK
    for i in range(CHUNK):
        part = slice(i * patch_rows, (i + 1) * patch_rows)
        place = pl.ds(pl.multiple_of(plan[turn + i], patch_rows), patch_rows)

        @pl.when(active)
        def _():
            kv_out[0, place, :] = keys_new[part]
            kv_out[1, place, :] = values_new[part]

        for h in range(local_width // head_dim):
            cols = slice(h * head_dim, (h + 1) * head_dim)
            scores = lax.dot_general(
                queries[h][part], kv_out[0, :, cols], (((1,), (1,)), ((), ())),
                preferred_element_type=F32,
            ) * (1.0 / math.sqrt(head_dim))
            weights = jnp.exp(scores - jnp.max(scores, axis=-1, keepdims=True))
            weights = weights / jnp.sum(weights, axis=-1, keepdims=True)
            mixture = jnp.dot(
                weights.astype(BF16), kv_out[1, :, cols], preferred_element_type=F32
            )
            mixture_out[part, cols] = mixture.astype(BF16)
    if finishes:
        for cols in blocks:
            terms = jnp.dot(mixture_out[...], w_last[:, cols], preferred_element_type=F32)
            for i in range(CHUNK):
                for g in range(terms_out.shape[0]):
                    at = i * patch_rows + g * shard_rows
                    terms_out[g, i, :, cols] = terms[at : at + shard_rows].astype(BF16)


def block_call(tick, sections, patch_rows, plan, gain, qk_gain, w_project, kv_state, kept,
               before=(), first=(), entry=None, last=()):
    width = gain.shape[1]
    local_width = kv_state.shape[2]
    rows = CHUNK * patch_rows
    macs = rows * width * local_width * 3
    out_shape = [
        jax.ShapeDtypeStruct((rows, width), BF16),
        jax.ShapeDtypeStruct((rows, local_width), BF16),
        jax.ShapeDtypeStruct(kv_state.shape, kv_state.dtype),
        jax.ShapeDtypeStruct(kept.shape, kept.dtype),
    ]
    if last:
        out_shape.append(
            jax.ShapeDtypeStruct((patch_rows // kept.shape[2],) + kept.shape[1:], BF16)
        )
    scratch = [pltpu.VMEM((rows, width), BF16), pltpu.VMEM((rows, width), F32)]
    if before:
        full = before[2].shape[0]
        macs += rows * width * full
        scratch.append(pltpu.VMEM((rows, full), BF16))
    operands = (gain, qk_gain, w_project, kv_state, kept, *before, *first, *last)
    return pl.pallas_call(
        lambda *refs: block_kernel(
            tick, sections, patch_rows, entry, bool(before), bool(last), *refs
        ),
        out_shape=out_shape,
        in_specs=[SMEM] + [VMEM] * len(operands),
        out_specs=[VMEM] * len(out_shape),
        scratch_shapes=scratch,
        compiler_params=pltpu.CompilerParams(vmem_limit_bytes=10 * MIB),
        cost_estimate=cost(macs, 2 * macs // rows),
    )(plan, *operands)


def close_kernel(sections, patch_rows, plan, terms, own, results, section_out):
    patches = section_out.shape[0]
    section_no = plan[patches]
    chunks = results.shape[0]
    for j in range(patches):
        section_out[plan[j] // patch_rows] = results[j // CHUNK, j % CHUNK]

    @pl.when(section_no == sections - 1)
    def _():
        for i in range(CHUNK):
            total = own[i].astype(F32)
            for g in range(terms.shape[0]):
                total += terms[g, i].astype(F32)
            section_out[plan[patches - CHUNK + i] // patch_rows] = total.astype(BF16)


def close_call(sections, patch_rows, plan, terms, own, results, shape):
    return pl.pallas_call(
        lambda *refs: close_kernel(sections, patch_rows, *refs),
        out_shape=jax.ShapeDtypeStruct(shape, BF16),
        in_specs=[SMEM, VMEM, VMEM, VMEM],
        out_specs=VMEM,
        compiler_params=pltpu.CompilerParams(vmem_limit_bytes=6 * MIB),
    )(plan, terms, own, results)


def on_device(latents, offsets, norm_gain, w_qkv, qk_gain, w_out, kv_cache):
    groups = lax.axis_size("sp")
    sections = lax.axis_size("section")
    section_no = lax.axis_index("section")
    group_no = lax.axis_index("sp")
    prompt_no = lax.axis_index("prompt")
    prompts = lax.axis_size("prompt")
    patches, shard_rows, width = latents.shape
    patch_rows = shard_rows * groups
    local_width = w_out.shape[1]
    chunks = patches // CHUNK
    plan = jnp.concatenate([offsets, jnp.stack([section_no, group_no]).astype(jnp.int32)])

    share = local_width // prompts
    own_share = lax.dynamic_slice_in_dim(w_out[0], prompt_no * share, share, 0)
    w_before = lax.all_gather(onward(own_share), ("sp", "prompt"), axis=0, tiled=True)
    w_project = jnp.swapaxes(w_qkv[0], 0, 1)

    ordered = order_call(patch_rows, plan, latents)
    entering = spread(ordered[:CHUNK])
    kv_state = kv_cache[0]
    kept = jnp.zeros((chunks, CHUNK, shard_rows, width), BF16)
    last_tick = chunks + sections - 2
    for tick in range(last_tick + 1):
        outs = block_call(
            tick, sections, patch_rows, plan, norm_gain, qk_gain[0], w_project, kv_state, kept,
            before=(gathered, x_before, w_before) if tick > 0 else (),
            first=(entering,) if tick < chunks else (),
            entry=(max(0, tick - 1) * CHUNK) if tick < chunks else None,
            last=(w_out[0],) if tick == last_tick else (),
        )
        x, mixture, kv_state, kept = outs[:4]
        if tick < last_tick:
            arrived = onward(mixture)
            arrived, x = lax.optimization_barrier((arrived, x))
            x_before = onward(x)
            gathered = spread(arrived)
        if tick == 0:
            rest, gathered = lax.optimization_barrier((ordered[CHUNK:], gathered))
            entering = spread(rest)

    terms = lax.all_to_all(outs[4], "sp", 0, 0)
    own = lax.dynamic_index_in_dim(
        x.reshape(CHUNK, groups, shard_rows, width), group_no, 1, keepdims=False
    )
    results = onward(kept, -1)
    section_out = close_call(sections, patch_rows, plan, terms, own, results, latents.shape)
    return section_out[None], kv_state[None]


def solution(mesh):
    in_specs = (
        P("prompt", "sp", None),
        P("prompt"),
        P("section", None),
        P("section", None, None, "sp"),
        P("section", None, None),
        P("section", "sp", None),
        P("section", None, "prompt", "sp"),
    )
    out_specs = (P("section", "prompt", "sp", None), P("section", None, "prompt", "sp"))
    return jax.shard_map(
        on_device, mesh=mesh, in_specs=in_specs, out_specs=out_specs, check_vma=False
    )
```

time: 1990 us -> 416 us (0.21)
  waiting for transfers between devices: 1150 us -> 103 us
  blocking collectives: 531 us -> 155 us
  matrix products: 73.1 us -> 0 us
  Pallas kernels: 0 us -> 62.3 us
  loops' own time: 61.3 us -> 0 us
  other arithmetic: 40.8 us -> 0.73 us
  local copies, waits for them, and re-layouts: 42.4 us -> 20.9 us
    reduce_scatter x15 -> x0, waiting for transfers between devices: 1130 us -> none  [tick(): lax.psum_scatter(jnp.dot(mixture, w_output, preferred_element_type=jnp.fl...]
    all_gather x15 -> x0, blocking collectives: 531 us -> none  [tick(): lax.all_gather(normed, 'sp', axis=0, tiled=True)]
    all_to_all x0 -> x10, blocking collectives: none -> 155 us  [spread(): return lax.all_to_all(copies, 'sp', 0, 0)]
    dot_general x60 -> x0, matrix products: 73.1 us -> none  [the longest x15 48.7 us: tick(): jnp.dot(lax.all_gather(normed, 'sp', axis=0, tiled=True), w_project, pref...]
    pallas_call x0 -> x13, Pallas kernels: none -> 62.3 us  [the longest x11 60.4 us: block_call(): pl.pallas_call(lambda *refs: block_kernel(tick, sections, patch_rows, ent...]
    another operation x1 -> x0, loops' own time: 61.3 us -> none  [on_device(): carry = lax.fori_loop(0, patch_count + section_count - 1, tick, carry)]
    all_to_all x0 -> x3, waiting for transfers between devices: none -> 38.8 us  [the longest x2 36.3 us: spread(): return lax.all_to_all(copies, 'sp', 0, 0)]
    ppermute x15 -> x22, waiting for transfers between devices: 25.9 us -> 63.7 us  [onward(): lax.ppermute(value, 'section', [(i, (i + steps) % count) for i in range(c...]
  transfers between devices with their start and end apart: 30 -> 26, of which waited for: 30 -> 16; matrix products, arithmetic and copies ran while one was open for 0% -> 1% of each run, Pallas kernels for 0% -> 1%
where the time goes in v1:
time: 416 us; the launch traced here: 408 us
  blocking collectives  155 us (37%)
  waiting for transfers between devices  103 us (25%)
  Pallas kernels  62.3 us (15%)
  starting transfers between devices  51 us (12%)
  local copies, waits for them, and re-layouts  20.9 us (5%)
  between operations  14.8 us (4%)
    all_to_all x10, blocking collectives, spread(): return lax.all_to_all(copies, 'sp', 0, 0)  155 us
    ppermute x22, waiting for transfers between devices, onward(): lax.ppermute(value, 'section', [(i, (i + steps) % count) for i in range(c...  63.7 us
    pallas_call x11, Pallas kernels, block_call(): pl.pallas_call(lambda *refs: block_kernel(tick, sections, patch_rows, ent...  60.4 us
    ppermute x22, starting transfers between devices, onward(): lax.ppermute(value, 'section', [(i, (i + steps) % count) for i in range(c...  40.2 us
    all_to_all x2, waiting for transfers between devices, spread(): return lax.all_to_all(copies, 'sp', 0, 0)  36.3 us
    unnamed x38, local copies, waits for them, and re-layouts  16.8 us
  transfers between devices with their start and end apart: 26, of which 16 were waited for; matrix products, arithmetic and copies ran while one was open for 1% of the time, Pallas kernels for 1%

profile of v1, /device:TPU:96, one launch (start us, length us, event | category | flops | bytes accessed | tf_op | source)
XLA Modules:
  0.0 407.6 jit_solution(7243810472853822410)
XLA Ops:
  11.5 8.4 %collective-permute-done.2 = bf16[64,3072]{1,0:T(8,128)(2,1)S(1)} collective-permute-done((bf16[64,3072]{1,0:T(8,128)(2,1)S(1)}, bf16[64,3072]{1,0:T(8,128)(2,1)S(1)}, u32[]{:S(2)}, u32[]{:S(2)}) %collective-permute-start.2) | collective-permute-done | bytes 393248 | tf_op jit(solution)/shard_map/ppermute | solution.py:21
  23.1 22.5 %all_to_all.65.refs_6_ = bf16[8,2,8,3072]{3,2,1,0:T(8,128)(2,1)S(1)} all-to-all(bf16[8,2,8,3072]{3,2,1,0:T(8,128)(2,1)S(1)} %broadcast_in_dim.31), channel_id=1, replica_groups=mesh['section'=8,'sp'=8,'prompt'=4] {'sp'}, dimensions={0} | all-to-all | bytes 1572864 | tf_op jit(solution)/shard_map/all_to_all | solution.py:27
  64.9 16.4 %all-to-all-done.1.refs_6_ = bf16[8,128,256]{2,1,0:T(8,128)(2,1)S(1)} async-done(((bf16[8,128,256]{2,1,0:T(8,128)(2,1)}), bf16[8,128,256]{2,1,0:T(8,128)(2,1)S(1)}, u32[]{:S(2)}, u32[]{:S(2)}) %all-to-all-start.1) | async-done | bytes 524320 | tf_op jit(solution)/shard_map/all_to_all | solution.py:27
  90.5 9.8 %collective-permute-done.1.refs_7_ = bf16[128,3072]{1,0:T(8,128)(2,1)S(1)} collective-permute-done((bf16[128,3072]{1,0:T(8,128)(2,1)}, bf16[128,3072]{1,0:T(8,128)(2,1)S(1)}, u32[]{:S(2)}, u32[]{:S(2)}) %collective-permute-start.1) | collective-permute-done | bytes 786464 | tf_op jit(solution)/shard_map/ppermute | solution.py:21
  101.3 19.9 %all-to-all-done.2.refs_9_ = bf16[8,6,8,3072]{3,2,1,0:T(8,128)(2,1)S(1)} async-done(((bf16[8,6,8,3072]{3,2,1,0:T(8,128)(2,1)}), bf16[8,6,8,3072]{3,2,1,0:T(8,128)(2,1)S(1)}, u32[]{:S(2)}, u32[]{:S(2)}) %all-to-all-start.2) | async-done | bytes 2359328 | tf_op jit(solution)/shard_map/all_to_all | solution.py:27
  131.2 5.6 %shard_map.88 = (bf16[128,3072]{1,0:T(8,128)(2,1)S(1)}, bf16[128,256]{1,0:T(8,128)(2,1)S(1)}, bf16[2,512,256]{2,1,0:T(8,128)(2,1)S(1)}, bf16[4,2,8,3072]{3,2,1,0:T(8,128)(2,1)S(1)}) custom-call(s32[10]{0:T(128)S(1)} %pad_add_fusion.refs_0_, f32[1,3072]{1,0:T(1,128)S(1)} %copy-done.5, f32[2,128]{1,0:T(2,128)S(1)} %bitcast.33, ...), custom_call_target="tpu_custom_call" | custom-call | flops 2214592512 | bytes 17301504 | tf_op jit(solution)/shard_map/pallas_call | solution.py:183
  146.0 13.1 %all_to_all.66.refs_6_ = bf16[8,128,256]{2,1,0:T(8,128)(2,1)S(1)} all-to-all(bf16[8,128,256]{2,1,0:T(8,128)(2,1)S(1)} %broadcast_in_dim.34), channel_id=1, replica_groups=mesh['section'=8,'sp'=8,'prompt'=4] {'sp'}, dimensions={0} | all-to-all | bytes 1048576 | tf_op jit(solution)/shard_map/all_to_all | solution.py:27
  159.1 5.5 %shard_map.89 = (bf16[128,3072]{1,0:T(8,128)(2,1)S(1)}, bf16[128,256]{1,0:T(8,128)(2,1)S(1)}, bf16[2,512,256]{2,1,0:T(8,128)(2,1)S(1)}, bf16[4,2,8,3072]{3,2,1,0:T(8,128)(2,1)S(1)}) custom-call(s32[10]{0:T(128)S(1)} %pad_add_fusion.refs_0_, f32[1,3072]{1,0:T(1,128)S(1)} %copy-done.5, f32[2,128]{1,0:T(2,128)S(1)} %bitcast.34, ...), custom_call_target="tpu_custom_call" | custom-call | flops 2214592512 | bytes 17301504 | tf_op jit(solution)/shard_map/pallas_call | solution.py:183
  172.5 16.1 %all_to_all.67.refs_6_ = bf16[8,128,256]{2,1,0:T(8,128)(2,1)S(1)} all-to-all(bf16[8,128,256]{2,1,0:T(8,128)(2,1)S(1)} %broadcast_in_dim.35), channel_id=1, replica_groups=mesh['section'=8,'sp'=8,'prompt'=4] {'sp'}, dimensions={0} | all-to-all | bytes 1048576 | tf_op jit(solution)/shard_map/all_to_all | solution.py:27
  188.6 5.5 %shard_map.90 = (bf16[128,3072]{1,0:T(8,128)(2,1)S(1)}, bf16[128,256]{1,0:T(8,128)(2,1)S(1)}, bf16[2,512,256]{2,1,0:T(8,128)(2,1)S(1)}, bf16[4,2,8,3072]{3,2,1,0:T(8,128)(2,1)S(1)}) custom-call(s32[10]{0:T(128)S(1)} %pad_add_fusion.refs_0_, f32[1,3072]{1,0:T(1,128)S(1)} %copy-done.5, f32[2,128]{1,0:T(2,128)S(1)} %bitcast.35, ...), custom_call_target="tpu_custom_call" | custom-call | flops 2214592512 | bytes 17301504 | tf_op jit(solution)/shard_map/pallas_call | solution.py:183
  200.5 17.7 %all_to_all.68.refs_6_ = bf16[8,128,256]{2,1,0:T(8,128)(2,1)S(1)} all-to-all(bf16[8,128,256]{2,1,0:T(8,128)(2,1)S(1)} %broadcast_in_dim.36), channel_id=1, replica_groups=mesh['section'=8,'sp'=8,'prompt'=4] {'sp'}, dimensions={0} | all-to-all | bytes 1048576 | tf_op jit(solution)/shard_map/all_to_all | solution.py:27
  218.2 5.5 %shard_map.91 = (bf16[128,3072]{1,0:T(8,128)(2,1)S(1)}, bf16[128,256]{1,0:T(8,128)(2,1)S(1)}, bf16[2,512,256]{2,1,0:T(8,128)(2,1)S(1)}, bf16[4,2,8,3072]{3,2,1,0:T(8,128)(2,1)S(1)}) custom-call(s32[10]{0:T(128)S(1)} %pad_add_fusion.refs_0_, f32[1,3072]{1,0:T(1,128)S(1)} %copy-done.5, f32[2,128]{1,0:T(2,128)S(1)} %bitcast.36, ...), custom_call_target="tpu_custom_call" | custom-call | flops 2214592512 | bytes 17301504 | tf_op jit(solution)/shard_map/pallas_call | solution.py:183
  230.1 15.5 %all_to_all.69.refs_6_ = bf16[8,128,256]{2,1,0:T(8,128)(2,1)S(1)} all-to-all(bf16[8,128,256]{2,1,0:T(8,128)(2,1)S(1)} %broadcast_in_dim.37), channel_id=1, replica_groups=mesh['section'=8,'sp'=8,'prompt'=4] {'sp'}, dimensions={0} | all-to-all | bytes 1048576 | tf_op jit(solution)/shard_map/all_to_all | solution.py:27
  245.6 5.5 %shard_map.92 = (bf16[128,3072]{1,0:T(8,128)(2,1)S(1)}, bf16[128,256]{1,0:T(8,128)(2,1)S(1)}, bf16[2,512,256]{2,1,0:T(8,128)(2,1)S(1)}, bf16[4,2,8,3072]{3,2,1,0:T(8,128)(2,1)S(1)}) custom-call(s32[10]{0:T(128)S(1)} %pad_add_fusion.refs_0_, f32[1,3072]{1,0:T(1,128)S(1)} %copy-done.5, f32[2,128]{1,0:T(2,128)S(1)} %bitcast.37, ...), custom_call_target="tpu_custom_call" | custom-call | flops 2214592512 | bytes 17301504 | tf_op jit(solution)/shard_map/pallas_call | solution.py:183
  257.5 13.5 %all_to_all.70.refs_6_ = bf16[8,128,256]{2,1,0:T(8,128)(2,1)S(1)} all-to-all(bf16[8,128,256]{2,1,0:T(8,128)(2,1)S(1)} %broadcast_in_dim.38), channel_id=1, replica_groups=mesh['section'=8,'sp'=8,'prompt'=4] {'sp'}, dimensions={0} | all-to-all | bytes 1048576 | tf_op jit(solution)/shard_map/all_to_all | solution.py:27
  271.0 5.8 %shard_map.93 = (bf16[128,3072]{1,0:T(8,128)(2,1)S(1)}, bf16[128,256]{1,0:T(8,128)(2,1)S(1)}, bf16[2,512,256]{2,1,0:T(8,128)(2,1)S(1)}, bf16[4,2,8,3072]{3,2,1,0:T(8,128)(2,1)S(1)}) custom-call(s32[10]{0:T(128)S(1)} %pad_add_fusion.refs_0_, f32[1,3072]{1,0:T(1,128)S(1)} %copy-done.5, f32[2,128]{1,0:T(2,128)S(1)} %bitcast.38, ...), custom_call_target="tpu_custom_call" | custom-call | flops 2214592512 | bytes 17301504 | tf_op jit(solution)/shard_map/pallas_call | solution.py:183
  283.5 13.5 %all_to_all.71.refs_6_ = bf16[8,128,256]{2,1,0:T(8,128)(2,1)S(1)} all-to-all(bf16[8,128,256]{2,1,0:T(8,128)(2,1)S(1)} %broadcast_in_dim.39), channel_id=1, replica_groups=mesh['section'=8,'sp'=8,'prompt'=4] {'sp'}, dimensions={0} | all-to-all | bytes 1048576 | tf_op jit(solution)/shard_map/all_to_all | solution.py:27
  297.0 5.5 %shard_map.94 = (bf16[128,3072]{1,0:T(8,128)(2,1)S(1)}, bf16[128,256]{1,0:T(8,128)(2,1)S(1)}, bf16[2,512,256]{2,1,0:T(8,128)(2,1)S(1)}, bf16[4,2,8,3072]{3,2,1,0:T(8,128)(2,1)S(1)}) custom-call(s32[10]{0:T(128)S(1)} %pad_add_fusion.refs_0_, f32[1,3072]{1,0:T(1,128)S(1)} %copy-done.5, f32[2,128]{1,0:T(2,128)S(1)} %bitcast.39, ...), custom_call_target="tpu_custom_call" | custom-call | flops 2214592512 | bytes 17301504 | tf_op jit(solution)/shard_map/pallas_call | solution.py:183
  308.5 13.5 %all_to_all.72.refs_6_ = bf16[8,128,256]{2,1,0:T(8,128)(2,1)S(1)} all-to-all(bf16[8,128,256]{2,1,0:T(8,128)(2,1)S(1)} %broadcast_in_dim.40), channel_id=1, replica_groups=mesh['section'=8,'sp'=8,'prompt'=4] {'sp'}, dimensions={0} | all-to-all | bytes 1048576 | tf_op jit(solution)/shard_map/all_to_all | solution.py:27
  333.6 13.5 %all_to_all.73.refs_6_ = bf16[8,128,256]{2,1,0:T(8,128)(2,1)S(1)} all-to-all(bf16[8,128,256]{2,1,0:T(8,128)(2,1)S(1)} %broadcast_in_dim.41), channel_id=1, replica_groups=mesh['section'=8,'sp'=8,'prompt'=4] {'sp'}, dimensions={0} | all-to-all | bytes 1048576 | tf_op jit(solution)/shard_map/all_to_all | solution.py:27
  347.2 5.5 %shard_map.96 = (bf16[128,3072]{1,0:T(8,128)(2,1)S(1)}, bf16[128,256]{1,0:T(8,128)(2,1)S(1)}, bf16[2,512,256]{2,1,0:T(8,128)(2,1)S(1)}, bf16[4,2,8,3072]{3,2,1,0:T(8,128)(2,1)S(1)}) custom-call(s32[10]{0:T(128)S(1)} %pad_add_fusion.refs_0_, f32[1,3072]{1,0:T(1,128)S(1)} %copy-done.5, f32[2,128]{1,0:T(2,128)S(1)} %bitcast.41, ...), custom_call_target="tpu_custom_call" | custom-call | flops 2214592512 | bytes 17301504 | tf_op jit(solution)/shard_map/pallas_call | solution.py:183
  360.6 16.4 %all_to_all.74.refs_6_ = bf16[8,128,256]{2,1,0:T(8,128)(2,1)S(1)} all-to-all(bf16[8,128,256]{2,1,0:T(8,128)(2,1)S(1)} %broadcast_in_dim.42), channel_id=1, replica_groups=mesh['section'=8,'sp'=8,'prompt'=4] {'sp'}, dimensions={0} | all-to-all | bytes 1048576 | tf_op jit(solution)/shard_map/all_to_all | solution.py:27
  377.1 6.8 %shard_map.97 = (bf16[128,3072]{1,0:T(8,128)(2,1)S(1)}, bf16[128,256]{1,0:T(8,128)(2,1)}, bf16[2,512,256]{2,1,0:T(8,128)(2,1)}, bf16[4,2,8,3072]{3,2,1,0:T(8,128)(2,1)S(1)}, bf16[8,2,8,3072]{3,2,1,0:T(8,128)(2,1)}) custom-call(s32[10]{0:T(128)S(1)} %pad_add_fusion.refs_0_, f32[1,3072]{1,0:T(1,128)S(1)} %copy-done.5, f32[2,128]{1,0:T(2,128)S(1)} %bitcast.42, ...), custom_call_target="tpu_custom_call" | custom-call | flops 2214592512 | bytes 17301504 | tf_op jit(solution)/shard_map/pallas_call | solution.py:183
  387.6 8.9 %collective-permute-done.21.refs_3_ = bf16[4,2,8,3072]{3,2,1,0:T(8,128)(2,1)S(1)} collective-permute-done((bf16[4,2,8,3072]{3,2,1,0:T(8,128)(2,1)S(1)}, bf16[4,2,8,3072]{3,2,1,0:T(8,128)(2,1)S(1)}, u32[]{:S(2)}, u32[]{:S(2)}) %collective-permute-start.21) | collective-permute-done | bytes 393248 | tf_op jit(solution)/shard_map/ppermute | solution.py:21
  (109 shorter events, 122.6 us)
Async XLA Ops:
  7.2 114.0 %all-gather.2.cloned.1.call-start = ((), (), s32[]{:S(2)}) async-start(), calls=%async_computation.13 | async-start | bytes 12976128 | tf_op jit(solution)/shard_map/all_gather | solution.py:237
  8.3 11.6 %collective-permute-start.2 = (bf16[64,3072]{1,0:T(8,128)(2,1)S(1)}, bf16[64,3072]{1,0:T(8,128)(2,1)S(1)}, u32[]{:S(2)}, u32[]{:S(2)}) collective-permute-start(bf16[64,3072]{1,0:T(8,128)(2,1)S(1)} %dynamic-slice_bitcast_fusion), channel_id=1, source_target_pairs={{0,32},{32,64},{64,96},{96,128},{128,160},{160,192},{192,224},{224... | collective-permute-start | bytes 1179656 | tf_op jit(solution)/shard_map/ppermute | solution.py:21
  53.3 7.2 %collective-permute-start = (bf16[128,256]{1,0:T(8,128)(2,1)S(1)}, bf16[128,256]{1,0:T(8,128)(2,1)S(1)}, u32[]{:S(2)}, u32[]{:S(2)}) collective-permute-start(bf16[128,256]{1,0:T(8,128)(2,1)S(1)} %get-tuple-element.70), channel_id=1, source_target_pairs={{0,32},{32,64},{64,96},{96,128},{128,160},{160,192},{192,224},{224... | collective-permute-start | bytes 196616 | tf_op jit(solution)/shard_map/ppermute | solution.py:21
  61.4 19.9 %all-to-all-start.1 = ((bf16[8,128,256]{2,1,0:T(8,128)(2,1)}), bf16[8,128,256]{2,1,0:T(8,128)(2,1)S(1)}, u32[]{:S(2)}, u32[]{:S(2)}) async-start(bf16[8,128,256]{2,1,0:T(8,128)(2,1)} %broadcast_in_dim.32), calls=%async_computation.1 | async-start | bytes 1048576 | tf_op jit(solution)/shard_map/all_to_all | solution.py:27
  83.0 38.1 %all-to-all-start.2 = ((bf16[8,6,8,3072]{3,2,1,0:T(8,128)(2,1)}), bf16[8,6,8,3072]{3,2,1,0:T(8,128)(2,1)S(1)}, u32[]{:S(2)}, u32[]{:S(2)}) async-start(bf16[8,6,8,3072]{3,2,1,0:T(8,128)(2,1)} %broadcast_in_dim.33), calls=%async_computation.2 | async-start | bytes 4718592 | tf_op jit(solution)/shard_map/all_to_all | solution.py:27
  86.8 13.6 %collective-permute-start.1 = (bf16[128,3072]{1,0:T(8,128)(2,1)}, bf16[128,3072]{1,0:T(8,128)(2,1)S(1)}, u32[]{:S(2)}, u32[]{:S(2)}) collective-permute-start(bf16[128,3072]{1,0:T(8,128)(2,1)} %copy-done.15), channel_id=1, source_target_pairs={{0,32},{32,64},{64,96},{96,128},{128,160},{160,192},{192,224},{224... | collective-permute-start | bytes 2359304 | tf_op jit(solution)/shard_map/ppermute | solution.py:21
  136.8 5.4 %collective-permute-start.3 = (bf16[128,256]{1,0:T(8,128)(2,1)S(1)}, bf16[128,256]{1,0:T(8,128)(2,1)S(1)}, u32[]{:S(2)}, u32[]{:S(2)}) collective-permute-start(bf16[128,256]{1,0:T(8,128)(2,1)S(1)} %get-tuple-element.78), channel_id=1, source_target_pairs={{0,32},{32,64},{64,96},{96,128},{128,160},{160,192},{192,224},{224... | collective-permute-start | bytes 196616 | tf_op jit(solution)/shard_map/ppermute | solution.py:21
  142.2 16.8 %collective-permute-start.4 = (bf16[128,3072]{1,0:T(8,128)(2,1)S(1)}, bf16[128,3072]{1,0:T(8,128)(2,1)S(1)}, u32[]{:S(2)}, u32[]{:S(2)}) collective-permute-start(bf16[128,3072]{1,0:T(8,128)(2,1)S(1)} %get-tuple-element.81), channel_id=1, source_target_pairs={{0,32},{32,64},{64,96},{96,128},{128,160},{160,192},{192,224},{224... | collective-permute-start | bytes 2359304 | tf_op jit(solution)/shard_map/ppermute | solution.py:21
  164.6 5.1 %collective-permute-start.5 = (bf16[128,256]{1,0:T(8,128)(2,1)S(1)}, bf16[128,256]{1,0:T(8,128)(2,1)S(1)}, u32[]{:S(2)}, u32[]{:S(2)}) collective-permute-start(bf16[128,256]{1,0:T(8,128)(2,1)S(1)} %get-tuple-element.84), channel_id=1, source_target_pairs={{0,32},{32,64},{64,96},{96,128},{128,160},{160,192},{192,224},{224... | collective-permute-start | bytes 196616 | tf_op jit(solution)/shard_map/ppermute | solution.py:21
  169.7 19.0 %collective-permute-start.6 = (bf16[128,3072]{1,0:T(8,128)(2,1)S(1)}, bf16[128,3072]{1,0:T(8,128)(2,1)S(1)}, u32[]{:S(2)}, u32[]{:S(2)}) collective-permute-start(bf16[128,3072]{1,0:T(8,128)(2,1)S(1)} %get-tuple-element.87), channel_id=1, source_target_pairs={{0,32},{32,64},{64,96},{96,128},{128,160},{160,192},{192,224},{224... | collective-permute-start | bytes 2359304 | tf_op jit(solution)/shard_map/ppermute | solution.py:21
  194.2 5.1 %collective-permute-start.7 = (bf16[128,256]{1,0:T(8,128)(2,1)S(1)}, bf16[128,256]{1,0:T(8,128)(2,1)S(1)}, u32[]{:S(2)}, u32[]{:S(2)}) collective-permute-start(bf16[128,256]{1,0:T(8,128)(2,1)S(1)} %get-tuple-element.90), channel_id=1, source_target_pairs={{0,32},{32,64},{64,96},{96,128},{128,160},{160,192},{192,224},{224... | collective-permute-start | bytes 196616 | tf_op jit(solution)/shard_map/ppermute | solution.py:21
  199.3 18.9 %collective-permute-start.8 = (bf16[128,3072]{1,0:T(8,128)(2,1)S(1)}, bf16[128,3072]{1,0:T(8,128)(2,1)S(1)}, u32[]{:S(2)}, u32[]{:S(2)}) collective-permute-start(bf16[128,3072]{1,0:T(8,128)(2,1)S(1)} %get-tuple-element.93), channel_id=1, source_target_pairs={{0,32},{32,64},{64,96},{96,128},{128,160},{160,192},{192,224},{224... | collective-permute-start | bytes 2359304 | tf_op jit(solution)/shard_map/ppermute | solution.py:21
  223.8 5.1 %collective-permute-start.9 = (bf16[128,256]{1,0:T(8,128)(2,1)S(1)}, bf16[128,256]{1,0:T(8,128)(2,1)S(1)}, u32[]{:S(2)}, u32[]{:S(2)}) collective-permute-start(bf16[128,256]{1,0:T(8,128)(2,1)S(1)} %get-tuple-element.96), channel_id=1, source_target_pairs={{0,32},{32,64},{64,96},{96,128},{128,160},{160,192},{192,224},{224... | collective-permute-start | bytes 196616 | tf_op jit(solution)/shard_map/ppermute | solution.py:21
  228.9 16.7 %collective-permute-start.10 = (bf16[128,3072]{1,0:T(8,128)(2,1)S(1)}, bf16[128,3072]{1,0:T(8,128)(2,1)S(1)}, u32[]{:S(2)}, u32[]{:S(2)}) collective-permute-start(bf16[128,3072]{1,0:T(8,128)(2,1)S(1)} %get-tuple-element.99), channel_id=1, source_target_pairs={{0,32},{32,64},{64,96},{96,128},{128,160},{160,192},{192,224},{224... | collective-permute-start | bytes 2359304 | tf_op jit(solution)/shard_map/ppermute | solution.py:21
  251.2 5.1 %collective-permute-start.11 = (bf16[128,256]{1,0:T(8,128)(2,1)S(1)}, bf16[128,256]{1,0:T(8,128)(2,1)S(1)}, u32[]{:S(2)}, u32[]{:S(2)}) collective-permute-start(bf16[128,256]{1,0:T(8,128)(2,1)S(1)} %get-tuple-element.102), channel_id=1, source_target_pairs={{0,32},{32,64},{64,96},{96,128},{128,160},{160,192},{192,224},{224... | collective-permute-start | bytes 196616 | tf_op jit(solution)/shard_map/ppermute | solution.py:21
  256.3 14.8 %collective-permute-start.12 = (bf16[128,3072]{1,0:T(8,128)(2,1)S(1)}, bf16[128,3072]{1,0:T(8,128)(2,1)S(1)}, u32[]{:S(2)}, u32[]{:S(2)}) collective-permute-start(bf16[128,3072]{1,0:T(8,128)(2,1)S(1)} %get-tuple-element.105), channel_id=1, source_target_pairs={{0,32},{32,64},{64,96},{96,128},{128,160},{160,192},{192,224},{224... | collective-permute-start | bytes 2359304 | tf_op jit(solution)/shard_map/ppermute | solution.py:21
  276.8 4.3 %collective-permute-start.13 = (bf16[128,256]{1,0:T(8,128)(2,1)S(1)}, bf16[128,256]{1,0:T(8,128)(2,1)S(1)}, u32[]{:S(2)}, u32[]{:S(2)}) collective-permute-start(bf16[128,256]{1,0:T(8,128)(2,1)S(1)} %get-tuple-element.108), channel_id=1, source_target_pairs={{0,32},{32,64},{64,96},{96,128},{128,160},{160,192},{192,224},{224... | collective-permute-start | bytes 196616 | tf_op jit(solution)/shard_map/ppermute | solution.py:21
  281.1 15.9 %collective-permute-start.14 = (bf16[128,3072]{1,0:T(8,128)(2,1)S(1)}, bf16[128,3072]{1,0:T(8,128)(2,1)S(1)}, u32[]{:S(2)}, u32[]{:S(2)}) collective-permute-start(bf16[128,3072]{1,0:T(8,128)(2,1)S(1)} %get-tuple-element.111), channel_id=1, source_target_pairs={{0,32},{32,64},{64,96},{96,128},{128,160},{160,192},{192,224},{224... | collective-permute-start | bytes 2359304 | tf_op jit(solution)/shard_map/ppermute | solution.py:21
  306.9 15.1 %collective-permute-start.16 = (bf16[128,3072]{1,0:T(8,128)(2,1)S(1)}, bf16[128,3072]{1,0:T(8,128)(2,1)S(1)}, u32[]{:S(2)}, u32[]{:S(2)}) collective-permute-start(bf16[128,3072]{1,0:T(8,128)(2,1)S(1)} %get-tuple-element.117), channel_id=1, source_target_pairs={{0,32},{32,64},{64,96},{96,128},{128,160},{160,192},{192,224},{224... | collective-permute-start | bytes 2359304 | tf_op jit(solution)/shard_map/ppermute | solution.py:21
  327.4 4.6 %collective-permute-start.17 = (bf16[128,256]{1,0:T(8,128)(2,1)S(1)}, bf16[128,256]{1,0:T(8,128)(2,1)S(1)}, u32[]{:S(2)}, u32[]{:S(2)}) collective-permute-start(bf16[128,256]{1,0:T(8,128)(2,1)S(1)} %get-tuple-element.120), channel_id=1, source_target_pairs={{0,32},{32,64},{64,96},{96,128},{128,160},{160,192},{192,224},{224... | collective-permute-start | bytes 196616 | tf_op jit(solution)/shard_map/ppermute | solution.py:21
  332.0 15.2 %collective-permute-start.18 = (bf16[128,3072]{1,0:T(8,128)(2,1)S(1)}, bf16[128,3072]{1,0:T(8,128)(2,1)S(1)}, u32[]{:S(2)}, u32[]{:S(2)}) collective-permute-start(bf16[128,3072]{1,0:T(8,128)(2,1)S(1)} %get-tuple-element.123), channel_id=1, source_target_pairs={{0,32},{32,64},{64,96},{96,128},{128,160},{160,192},{192,224},{224... | collective-permute-start | bytes 2359304 | tf_op jit(solution)/shard_map/ppermute | solution.py:21
  357.1 20.0 %collective-permute-start.20 = (bf16[128,3072]{1,0:T(8,128)(2,1)S(1)}, bf16[128,3072]{1,0:T(8,128)(2,1)S(1)}, u32[]{:S(2)}, u32[]{:S(2)}) collective-permute-start(bf16[128,3072]{1,0:T(8,128)(2,1)S(1)} %get-tuple-element.129), channel_id=1, source_target_pairs={{0,32},{32,64},{64,96},{96,128},{128,160},{160,192},{192,224},{224... | collective-permute-start | bytes 2359304 | tf_op jit(solution)/shard_map/ppermute | solution.py:21
  383.9 15.1 %all-to-all-start.12 = ((bf16[8,2,8,3072]{3,2,1,0:T(8,128)(2,1)}), bf16[8,2,8,3072]{3,2,1,0:T(8,128)(2,1)S(1)}, u32[]{:S(2)}, u32[]{:S(2)}) async-start(bf16[8,2,8,3072]{3,2,1,0:T(8,128)(2,1)} %get-tuple-element.130), calls=%async_computation.12 | async-start | bytes 1572864 | tf_op jit(solution)/shard_map/all_to_all | solution.py:263
  387.5 9.1 %collective-permute-start.21 = (bf16[4,2,8,3072]{3,2,1,0:T(8,128)(2,1)S(1)}, bf16[4,2,8,3072]{3,2,1,0:T(8,128)(2,1)S(1)}, u32[]{:S(2)}, u32[]{:S(2)}) collective-permute-start(bf16[4,2,8,3072]{3,2,1,0:T(8,128)(2,1)S(1)} %get-tuple-element.132), channel_id=1, source_target_pairs={{0,224},{32,0},{64,32},{96,64},{128,96},{160,128},{192,160},{224,1... | collective-permute-start | bytes 1179656 | tf_op jit(solution)/shard_map/ppermute | solution.py:21
  (21 other events, 326.4 us)
Sparse Core Ops, SparseCore 0:
  20.8 94.6 all-gather.1
